TPU v7x, 32 devices: a whole 2x2x4 slice. The times are simulated.
32 devices in a mesh: ctx: 16 (over z, y, core), head: 2 (over x).
Axes of the slice: x: 2, y: 2, z: 4, core: 2. Of those that a mesh axis runs over, the one named last changes fastest.
Arguments:
- query_rows: bfloat16 [8192, 1536], P(('ctx', 'head')), may hold values from -51 to 51
- key_rows: bfloat16 [8192, 1536], P(('ctx', 'head')), may hold values from -6 to 6
- value_rows: bfloat16 [8192, 1536], P(('ctx', 'head')), may hold values from -12 to 12
- residual: bfloat16 [8192, 1536], P(('ctx', 'head')), may hold values from -6 to 6
- levels: int32 [16], P('ctx'), may hold values from 0 to 49
- gate_table: float32 [50, 1536], replicated, may hold values from -4 to 4
- block_mask: int32 [16, 7, 4, 4], P('ctx'), may hold values from 0 to 1, as said below
- out_weight: bfloat16 [1536, 1536], P('head'), may hold values from -0.15625 to 0.15625
Outputs:
- mixed: bfloat16 [8192, 1536], P(('ctx', 'head'))
Inputs may be any that keep to these rules, and one draw needn't show every extreme that they name: block_mask[f, s, a, b] = 1 lets query block a of frame f attend key block b of frame f + offset(s); slot 0 is all ones; entries whose frame f + offset(s) lies outside the clip are 0.
All inputs are finite; a program needn't handle non-finite values.
Results may differ from a plain program's by a relative error of at most 0.0065.
Values may be sent and summed in bfloat16 or wider, within the bound.
A program may use at most 64 MiB of HBM per device.

v0:
```python
import math

import jax
import jax.numpy as jnp
from jax import lax
from jax.sharding import PartitionSpec as P

HEAD_DIM = 128
BLOCK = 128
LOGR = 3


def from_behind(shard, axis, by):
    length = lax.axis_size(axis)
    pairs = [(i, i + by) for i in range(length) if 0 <= i + by < length]
    return lax.ppermute(shard, axis, pairs)


def expand_blocks(block_rows):
    blocks = block_rows.shape[0]
    broadened = jnp.broadcast_to(block_rows[:, None, :, None], (blocks, BLOCK, blocks, BLOCK))
    return broadened.reshape(blocks * BLOCK, blocks * BLOCK) > 0


def fold_slot(running, queries, key_values, allowed):
    run_max, run_total, run_acc = running
    scores = jnp.einsum("qhd,khd->hqk", queries, key_values[0], preferred_element_type=jnp.float32)
    scores = jnp.where(allowed[None], scores * (1.0 / math.sqrt(HEAD_DIM)), -jnp.inf)
    new_max = jnp.maximum(run_max, jnp.max(scores, axis=2))
    rescale = jnp.exp(run_max - new_max)
    exp_scores = jnp.exp(scores - new_max[:, :, None])
    run_total = run_total * rescale + jnp.sum(exp_scores, axis=2)
    weighted = jnp.einsum(
        "hqk,khd->qhd",
        exp_scores.astype(jnp.bfloat16),
        key_values[1],
        preferred_element_type=jnp.float32,
    )
    run_acc = run_acc * jnp.transpose(rescale)[:, :, None] + weighted
    return (new_max, run_total, run_acc)


def body(query_rows, key_rows, value_rows, residual, levels, gate_table, block_mask, out_weight):
    tok_count = query_rows.shape[0]
    heads_here = query_rows.shape[1] // HEAD_DIM
    shaped = [
        rows.reshape(tok_count, heads_here, HEAD_DIM) for rows in (query_rows, key_rows, value_rows)
    ]
    queries, keys_frame, values_frame = (
        lax.all_to_all(shaped[0], "head", split_axis=1, concat_axis=0, tiled=True),
        lax.all_to_all(shaped[1], "head", split_axis=1, concat_axis=0, tiled=True),
        lax.all_to_all(shaped[2], "head", split_axis=1, concat_axis=0, tiled=True),
    )
    key_values = jnp.stack([keys_frame, values_frame])
    pieces = [key_values] + [None] * (2 * LOGR)
    for octave in range(LOGR):
        for polarity in (0, 1):
            shift_by = 2**octave if polarity == 0 else -(2**octave)
            pieces[1 + 2 * octave + polarity] = from_behind(key_values, "ctx", shift_by)
    frame_len = queries.shape[0]
    group_heads = queries.shape[1]
    running = (
        jnp.full((group_heads, frame_len), -jnp.inf, jnp.float32),
        jnp.zeros((group_heads, frame_len), jnp.float32),
        jnp.zeros((frame_len, group_heads, HEAD_DIM), jnp.float32),
    )
    for slot_idx in range(2 * LOGR + 1):
        running = fold_slot(
            running, queries, pieces[slot_idx], expand_blocks(block_mask[0, slot_idx])
        )
    attention = (running[2] / jnp.transpose(running[1])[:, :, None]).astype(jnp.bfloat16)
    gate_row = lax.dynamic_index_in_dim(gate_table, levels[0], 0, keepdims=False)
    tok_heads = lax.all_to_all(attention, "head", split_axis=0, concat_axis=1, tiled=True)
    gathered_tok = tok_heads.reshape(tok_heads.shape[0], -1)
    projected = jnp.dot(
        gathered_tok,
        lax.all_gather(out_weight, "head", axis=0, tiled=True),
        preferred_element_type=jnp.float32,
    )
    return (residual.astype(jnp.float32) + gate_row[None, :] * projected).astype(jnp.bfloat16)


def solution(mesh):
    return jax.shard_map(
        body,
        mesh=mesh,
        in_specs=(
            P(("ctx", "head"), None),
            P(("ctx", "head"), None),
            P(("ctx", "head"), None),
            P(("ctx", "head"), None),
            P("ctx"),
            P(),
            P("ctx", None, None, None),
            P("head", None),
        ),
        out_specs=P(("ctx", "head"), None),
        check_vma=False,
    )
```

profile of v0, /device:TPU:20, one launch (start us, length us, event | category | flops | bytes accessed | tf_op | source)
XLA Modules:
  0.0 231.6 jit_solution(2539029929176882223)
XLA Ops:
  6.5 2.4 %copy.118 = bf16[256,1536]{0,1:T(8,128)(2,1)} copy(bf16[256,1536]{1,0:T(8,128)(2,1)} %param.9) | data formatting | bytes 1572864 | tf_op args[1]
  8.9 3.5 %all-to-all-start.1 = ((bf16[256,12,128]{0,2,1:T(8,128)(2,1)}), bf16[256,12,128]{0,2,1:T(8,128)(2,1)S(1)}, u32[]{:S(2)}, u32[]{:S(2)}) async-start(bf16[256,12,128]{0,2,1:T(8,128)(2,1)} %bitcast.7), calls=%async_computation.1 | async-start | bytes 1572864 | tf_op jit(solution)/shard_map/all_to_all | solution.py:51
  14.8 8.7 %all-to-all-done.1 = bf16[256,12,128]{0,2,1:T(8,128)(2,1)S(1)} async-done(((bf16[256,12,128]{0,2,1:T(8,128)(2,1)}), bf16[256,12,128]{0,2,1:T(8,128)(2,1)S(1)}, u32[]{:S(2)}, u32[]{:S(2)}) %all-to-all-start.1) | async-done | bytes 786464 | tf_op jit(solution)/shard_map/all_to_all | solution.py:51
  23.5 3.5 %all-to-all-start.2 = ((bf16[256,12,128]{0,2,1:T(8,128)(2,1)}), bf16[256,12,128]{0,2,1:T(8,128)(2,1)S(1)}, u32[]{:S(2)}, u32[]{:S(2)}) async-start(bf16[256,12,128]{0,2,1:T(8,128)(2,1)} %bitcast.13), calls=%async_computation.2 | async-start | bytes 1572864 | tf_op jit(solution)/shard_map/all_to_all | solution.py:52
  28.2 9.0 %all-to-all-done.2 = bf16[256,12,128]{0,2,1:T(8,128)(2,1)S(1)} async-done(((bf16[256,12,128]{0,2,1:T(8,128)(2,1)}), bf16[256,12,128]{0,2,1:T(8,128)(2,1)S(1)}, u32[]{:S(2)}, u32[]{:S(2)}) %all-to-all-start.2) | async-done | bytes 786464 | tf_op jit(solution)/shard_map/all_to_all | solution.py:52
  37.2 3.5 %all-to-all-start = ((bf16[256,12,128]{0,2,1:T(8,128)(2,1)}), bf16[256,12,128]{0,2,1:T(8,128)(2,1)S(1)}, u32[]{:S(2)}, u32[]{:S(2)}) async-start(bf16[256,12,128]{0,2,1:T(8,128)(2,1)} %bitcast.2), calls=%async_computation | async-start | bytes 1572864 | tf_op jit(solution)/shard_map/all_to_all | solution.py:50
  56.4 2.4 %collective-permute-start.3 = (bf16[2,512,6,128]{3,1,2,0:T(8,128)(2,1)}, bf16[2,512,6,128]{3,1,2,0:T(8,128)(2,1)}, u32[]{:S(2)}, u32[]{:S(2)}) collective-permute-start(bf16[2,512,6,128]{3,1,2,0:T(8,128)(2,1)} %pad_maximum_fusion), channel_id=1, source_target_pairs={{4,0},{6,2},{8,4},{10,6},{12,8},{14,10},{16,12},{18,14},{20,16},{2... | collective-permute-start | bytes 4718600 | tf_op jit(solution)/shard_map/ppermute | solution.py:16
  58.8 4.3 %collective-permute-start.2 = (bf16[2,512,6,128]{3,1,2,0:T(8,128)(2,1)}, bf16[2,512,6,128]{3,1,2,0:T(8,128)(2,1)}, u32[]{:S(2)}, u32[]{:S(2)}) collective-permute-start(bf16[2,512,6,128]{3,1,2,0:T(8,128)(2,1)} %pad_maximum_fusion), channel_id=1, source_target_pairs={{0,4},{2,6},{4,8},{6,10},{8,12},{10,14},{12,16},{14,18},{16,20},{1... | collective-permute-start | bytes 4718600 | tf_op jit(solution)/shard_map/ppermute | solution.py:16
  67.6 3.1 %fusion.21 = f32[6,512,128]{2,1,0:T(8,128)} fusion(bf16[512,6,128]{2,0,1:T(8,128)(2,1)S(1)} %bitcast.368, f32[6,512,512]{1,2,0:T(8,128)S(1)} %get-tuple-element.38, f32[6,512]{1,0:T(8,128)S(1)} %get-tuple-element.37, pred[512,512]{0,1:T(8,128)(4,1)S(1)} %bitcast.388), kind=kOutput, calls=%fused_computation.35 | convolution fusion | flops 408944640 | bytes 8925184 | tf_op jit(solution)/shard_map/hqk,khd->qhd/dot_general | solution.py:33
  72.7 5.9 %collective-permute-start.4 = (bf16[2,512,6,128]{3,1,2,0:T(8,128)(2,1)}, bf16[2,512,6,128]{3,1,2,0:T(8,128)(2,1)S(1)}, u32[]{:S(2)}, u32[]{:S(2)}) collective-permute-start(bf16[2,512,6,128]{3,1,2,0:T(8,128)(2,1)} %pad_maximum_fusion), channel_id=1, source_target_pairs={{0,8},{2,10},{4,12},{6,14},{8,16},{10,18},{12,20},{14,22},{16,24},... | collective-permute-start | bytes 4718600 | tf_op jit(solution)/shard_map/ppermute | solution.py:16
  80.9 68.0 %collective-permute-done.1 = bf16[2,512,6,128]{3,1,2,0:T(8,128)(2,1)} collective-permute-done((bf16[2,512,6,128]{3,1,2,0:T(8,128)(2,1)}, bf16[2,512,6,128]{3,1,2,0:T(8,128)(2,1)}, u32[]{:S(2)}, u32[]{:S(2)}) %collective-permute-start.1) | collective-permute-done | bytes 1572896 | tf_op jit(solution)/shard_map/ppermute | solution.py:16
  155.9 3.8 %fusion.19 = (f32[6,512]{1,0:T(8,128)S(1)}, f32[6,512,512]{2,1,0:T(8,128)}) fusion(pred[512,512]{0,1:T(8,128)(4,1)S(1)} %bitcast.376, bf16[512,6,128]{2,0,1:T(8,128)(2,1)S(1)} %bitcast.357, bf16[2,512,6,128]{3,1,2,0:T(8,128)(2,1)S(1)} %collective-permute-done.4), kind=kOutput, calls=%fused_computation.33 | convolution fusion | flops 407368704 | bytes 8138752 | tf_op jit(solution)/shard_map/qhd,khd->hqk/dot_general | solution.py:27
  162.6 5.3 %fusion.9 = (f32[6,512]{1,0:T(8,128)}, f32[6,512]{1,0:T(8,128)}) fusion(f32[6,512,512]{2,1,0:T(8,128)} %get-tuple-element.30, f32[6,512]{1,0:T(8,128)S(1)} %get-tuple-element.13, pred[512,512]{0,1:T(8,128)(4,1)S(1)} %bitcast.377, f32[6,512]{1,0:T(8,128)S(1)} %get-tuple-element.12, f32[6,512,512]{2,1,0:T(8,128)S(1)} %get-tuple-element.28, ...), kind=kLoop, calls=%fused_computation.23 | loop fusion | flops 12576768 | bytes 13156352 | tf_op jit(solution)/shard_map/reduce_sum | solution.py:32
  167.9 3.3 %fusion.5 = (f32[6,512]{1,0:T(8,128)}, f32[6,512]{1,0:T(8,128)}) fusion(f32[6,512,512]{2,1,0:T(8,128)S(1)} %get-tuple-element.34, f32[6,512]{1,0:T(8,128)S(1)} %get-tuple-element.15, pred[512,512]{0,1:T(8,128)(4,1)S(1)} %bitcast.382, f32[6,512]{1,0:T(8,128)S(1)} %get-tuple-element.14, f32[6,512,512]{2,1,0:T(8,128)S(1)} %get-tuple-element.32, ...), kind=kLoop, calls=%fused_computation.19 | loop fusion | flops 12576768 | bytes 13156352 | tf_op jit(solution)/shard_map/reduce_sum | solution.py:32
  171.1 4.6 %fusion.1 = (f32[6,512]{1,0:T(8,128)}, f32[6,512]{1,0:T(8,128)}) fusion(f32[6,512,512]{2,1,0:T(8,128)S(1)} %get-tuple-element.40, f32[6,512]{1,0:T(8,128)} %get-tuple-element.17, pred[512,512]{0,1:T(8,128)(4,1)} %bitcast.378, f32[6,512]{1,0:T(8,128)} %get-tuple-element.16, f32[6,512,512]{2,1,0:T(8,128)S(1)} %get-tuple-element.36, pred[512,512]{0,1:T(8,128)(4,1)} %bitcast.372), kind=kLoop, calls=%fused_computation.15 | loop fusion | flops 12576768 | bytes 13156352 | tf_op jit(solution)/shard_map/reduce_sum | solution.py:32
  177.9 4.3 %fusion.25 = f32[6,128,512]{1,2,0:T(8,128)} fusion(f32[6,512,512]{2,1,0:T(8,128)S(1)} %bitcast.360, f32[6,512]{1,0:T(8,128)} %copy-done.24, pred[512,512]{0,1:T(8,128)(4,1)} %bitcast.375, bf16[2,512,6,128]{3,1,2,0:T(8,128)(2,1)} %copy-done.15), kind=kOutput, calls=%fused_computation.37 | convolution fusion | flops 408944640 | bytes 8929280 | tf_op jit(solution)/shard_map/hqk,khd->qhd/dot_general | solution.py:33
  182.2 3.1 %fusion.27 = f32[6,128,512]{1,2,0:T(8,128)S(1)} fusion(f32[6,512,512]{2,1,0:T(8,128)S(1)} %get-tuple-element.32, f32[6,512]{1,0:T(8,128)S(1)} %copy-done.23, pred[512,512]{0,1:T(8,128)(4,1)} %bitcast.384, bf16[2,512,6,128]{3,1,2,0:T(8,128)(2,1)} %collective-permute-done.3), kind=kOutput, calls=%fused_computation.38 | convolution fusion | flops 408944640 | bytes 8925184 | tf_op jit(solution)/shard_map/hqk,khd->qhd/dot_general | solution.py:33
  185.4 3.1 %fusion.29 = f32[6,128,512]{1,2,0:T(8,128)S(1)} fusion(f32[6,512,512]{2,1,0:T(8,128)S(1)} %get-tuple-element.34, f32[6,512]{1,0:T(8,128)S(1)} %copy-done.21, pred[512,512]{0,1:T(8,128)(4,1)S(1)} %bitcast.383, bf16[2,512,6,128]{3,1,2,0:T(8,128)(2,1)} %collective-permute-done.2), kind=kOutput, calls=%fused_computation.39 | convolution fusion | flops 408944640 | bytes 8925184 | tf_op jit(solution)/shard_map/hqk,khd->qhd/dot_general | solution.py:33
  188.5 3.1 %fusion.31 = f32[6,128,512]{1,2,0:T(8,128)S(1)} fusion(f32[6,512,512]{2,1,0:T(8,128)S(1)} %get-tuple-element.36, f32[6,512]{1,0:T(8,128)S(1)} %copy-done.19, pred[512,512]{0,1:T(8,128)(4,1)S(1)} %bitcast.374, bf16[2,512,6,128]{3,1,2,0:T(8,128)(2,1)} %collective-permute-done.1), kind=kOutput, calls=%fused_computation.40 | convolution fusion | flops 408944640 | bytes 8925184 | tf_op jit(solution)/shard_map/hqk,khd->qhd/dot_general | solution.py:33
  191.7 3.2 %fusion.33 = f32[6,128,512]{1,2,0:T(8,128)S(1)} fusion(f32[6,512,512]{2,1,0:T(8,128)S(1)} %get-tuple-element.40, f32[6,512]{1,0:T(8,128)S(1)} %copy-done.18, pred[512,512]{0,1:T(8,128)(4,1)S(1)} %bitcast.380, bf16[2,512,6,128]{3,1,2,0:T(8,128)(2,1)} %collective-permute-done), kind=kOutput, calls=%fused_computation.41 | convolution fusion | flops 408944640 | bytes 8925184 | tf_op jit(solution)/shard_map/hqk,khd->qhd/dot_general | solution.py:33
  195.0 6.5 %fusion.66 = bf16[512,6,128]{2,0,1:T(8,128)(2,1)S(1)} fusion(f32[6,128,512]{1,2,0:T(8,128)S(1)} %copy-done.34, f32[6,128,512]{1,2,0:T(8,128)S(1)} %fusion.27, f32[6,128,512]{1,2,0:T(8,128)S(1)} %fusion.29, f32[6,128,512]{1,2,0:T(8,128)S(1)} %fusion.31, f32[6,128,512]{1,2,0:T(8,128)S(1)} %fusion.33, f32[6,512,128]{2,1,0:T(8,128)S(1)} %copy-done.35, ...), kind=kOutput, calls=%fused_computation.76 | convolution fusion | flops 414842880 | bytes 17674240 | tf_op jit(solution)/shard_map/hqk,khd->qhd/dot_general | solution.py:33
  203.1 3.6 %all-to-all-start.3 = ((bf16[512,6,128]{2,1,0:T(8,128)(2,1)}), bf16[512,6,128]{2,1,0:T(8,128)(2,1)S(1)}, u32[]{:S(2)}, u32[]{:S(2)}) async-start(bf16[512,6,128]{2,1,0:T(8,128)(2,1)} %copy.152), calls=%async_computation.3 | async-start | bytes 2097152 | tf_op jit(solution)/shard_map/all_to_all | solution.py:73
  207.3 12.1 %all-to-all-done.3 = bf16[512,6,128]{2,1,0:T(8,128)(2,1)S(1)} async-done(((bf16[512,6,128]{2,1,0:T(8,128)(2,1)}), bf16[512,6,128]{2,1,0:T(8,128)(2,1)S(1)}, u32[]{:S(2)}, u32[]{:S(2)}) %all-to-all-start.3) | async-done | bytes 786464 | tf_op jit(solution)/shard_map/all_to_all | solution.py:73
  220.1 4.6 %fusion.64 = bf16[256,1536]{1,0:T(8,128)(2,1)} fusion(bf16[256,1536]{0,1:T(8,128)(2,1)S(1)} %bitcast.397, bf16[1536,1536]{1,0:T(8,128)(2,1)} %all-gather.2.cloned.1.call-done, bf16[256,1536]{1,0:T(8,128)(2,1)S(1)} %copy-done.33, f32[1536]{0:T(1024)S(1)} %dynamic-slice_reduce_fusion), kind=kOutput, calls=%fused_computation.72 | convolution fusion | flops 1209532416 | bytes 7084032 | tf_op jit(solution)/shard_map/dot_general | solution.py:75
  (130 shorter events, 41.8 us)
Async XLA Ops:
  6.5 200.8 %copy-start = (f32[50,1536]{1,0:T(8,128)S(1)}, f32[50,1536]{1,0:T(8,128)}, u32[]{:S(2)}) copy-start(f32[50,1536]{1,0:T(8,128)} %param.13) | copy-start | bytes 921604
  6.5 20.5 %copy-start.13 = (bf16[256,1536]{1,0:T(8,128)(2,1)S(1)}, bf16[256,1536]{1,0:T(8,128)(2,1)}, u32[]{:S(2)}) copy-start(bf16[256,1536]{1,0:T(8,128)(2,1)} %param.8) | copy-start | bytes 2359300
  8.9 14.6 %all-to-all-start.1 = ((bf16[256,12,128]{0,2,1:T(8,128)(2,1)}), bf16[256,12,128]{0,2,1:T(8,128)(2,1)S(1)}, u32[]{:S(2)}, u32[]{:S(2)}) async-start(bf16[256,12,128]{0,2,1:T(8,128)(2,1)} %bitcast.7), calls=%async_computation.1 | async-start | bytes 1572864 | tf_op jit(solution)/shard_map/all_to_all | solution.py:51
  23.5 13.7 %all-to-all-start.2 = ((bf16[256,12,128]{0,2,1:T(8,128)(2,1)}), bf16[256,12,128]{0,2,1:T(8,128)(2,1)S(1)}, u32[]{:S(2)}, u32[]{:S(2)}) async-start(bf16[256,12,128]{0,2,1:T(8,128)(2,1)} %bitcast.13), calls=%async_computation.2 | async-start | bytes 1572864 | tf_op jit(solution)/shard_map/all_to_all | solution.py:52
  27.1 18.5 %copy-start.14 = (s32[1,7,4,4]{1,3,2,0:T(4,128)S(1)}, s32[1,7,4,4]{1,3,2,0:T(4,128)}, u32[]{:S(2)}) copy-start(s32[1,7,4,4]{1,3,2,0:T(4,128)} %param.14) | copy-start | bytes 1348
  37.2 27.8 %all-to-all-start = ((bf16[256,12,128]{0,2,1:T(8,128)(2,1)}), bf16[256,12,128]{0,2,1:T(8,128)(2,1)S(1)}, u32[]{:S(2)}, u32[]{:S(2)}) async-start(bf16[256,12,128]{0,2,1:T(8,128)(2,1)} %bitcast.2), calls=%async_computation | async-start | bytes 1572864 | tf_op jit(solution)/shard_map/all_to_all | solution.py:50
  40.8 179.3 %all-gather.2.cloned.1.call-start = ((), (), s32[]{:S(2)}) async-start(), calls=%async_computation.4 | async-start | bytes 7077888 | tf_op jit(solution)/shard_map/all_gather | solution.py:77
  42.3 22.8 %copy-start.1 = (bf16[2,256,6,128]{3,1,0,2:T(8,128)(2,1)}, bf16[2,256,6,128]{3,1,0,2:T(8,128)(2,1)S(1)}, u32[]{:S(2)}) copy-start(bf16[2,256,6,128]{3,1,0,2:T(8,128)(2,1)S(1)} %copy.124) | copy-start | bytes 2359300
  43.7 29.0 %collective-permute-start = (bf16[2,512,6,128]{3,1,2,0:T(8,128)(2,1)}, bf16[2,512,6,128]{3,1,2,0:T(8,128)(2,1)}, u32[]{:S(2)}, u32[]{:S(2)}) collective-permute-start(bf16[2,512,6,128]{3,1,2,0:T(8,128)(2,1)} %pad_maximum_fusion), channel_id=1, source_target_pairs={{0,2},{2,4},{4,6},{6,8},{8,10},{10,12},{12,14},{14,16},{16,18},{18... | collective-permute-start | bytes 4718600 | tf_op jit(solution)/shard_map/ppermute | solution.py:16
  54.0 105.7 %collective-permute-start.5 = (bf16[2,512,6,128]{3,1,2,0:T(8,128)(2,1)}, bf16[2,512,6,128]{3,1,2,0:T(8,128)(2,1)}, u32[]{:S(2)}, u32[]{:S(2)}) collective-permute-start(bf16[2,512,6,128]{3,1,2,0:T(8,128)(2,1)} %pad_maximum_fusion), channel_id=1, source_target_pairs={{8,0},{10,2},{12,4},{14,6},{16,8},{18,10},{20,12},{22,14},{24,16},... | collective-permute-start | bytes 4718600 | tf_op jit(solution)/shard_map/ppermute | solution.py:16
  56.4 97.2 %collective-permute-start.3 = (bf16[2,512,6,128]{3,1,2,0:T(8,128)(2,1)}, bf16[2,512,6,128]{3,1,2,0:T(8,128)(2,1)}, u32[]{:S(2)}, u32[]{:S(2)}) collective-permute-start(bf16[2,512,6,128]{3,1,2,0:T(8,128)(2,1)} %pad_maximum_fusion), channel_id=1, source_target_pairs={{4,0},{6,2},{8,4},{10,6},{12,8},{14,10},{16,12},{18,14},{20,16},{2... | collective-permute-start | bytes 4718600 | tf_op jit(solution)/shard_map/ppermute | solution.py:16
  58.8 92.4 %collective-permute-start.2 = (bf16[2,512,6,128]{3,1,2,0:T(8,128)(2,1)}, bf16[2,512,6,128]{3,1,2,0:T(8,128)(2,1)}, u32[]{:S(2)}, u32[]{:S(2)}) collective-permute-start(bf16[2,512,6,128]{3,1,2,0:T(8,128)(2,1)} %pad_maximum_fusion), channel_id=1, source_target_pairs={{0,4},{2,6},{4,8},{6,10},{8,12},{10,14},{12,16},{14,18},{16,20},{1... | collective-permute-start | bytes 4718600 | tf_op jit(solution)/shard_map/ppermute | solution.py:16
  63.1 85.8 %collective-permute-start.1 = (bf16[2,512,6,128]{3,1,2,0:T(8,128)(2,1)}, bf16[2,512,6,128]{3,1,2,0:T(8,128)(2,1)}, u32[]{:S(2)}, u32[]{:S(2)}) collective-permute-start(bf16[2,512,6,128]{3,1,2,0:T(8,128)(2,1)} %pad_maximum_fusion), channel_id=1, source_target_pairs={{2,0},{4,2},{6,4},{8,6},{10,8},{12,10},{14,12},{16,14},{18,16},{20... | collective-permute-start | bytes 4718600 | tf_op jit(solution)/shard_map/ppermute | solution.py:16
  67.6 11.0 %copy-start.7 = (pred[64,8,4,128]{3,1,2,0:T(8,128)(4,1)S(1)}, pred[64,8,4,128]{3,1,2,0:T(8,128)(4,1)}, u32[]{:S(2)}) copy-start(pred[64,8,4,128]{3,1,2,0:T(8,128)(4,1)} %copy.206) | copy-start | bytes 786436
  70.7 78.2 %copy-start.4 = (pred[64,8,4,128]{3,1,2,0:T(8,128)(4,1)S(1)}, pred[64,8,4,128]{3,1,2,0:T(8,128)(4,1)}, u32[]{:S(2)}) copy-start(pred[64,8,4,128]{3,1,2,0:T(8,128)(4,1)} %copy.205) | copy-start | bytes 786436
  72.7 83.2 %collective-permute-start.4 = (bf16[2,512,6,128]{3,1,2,0:T(8,128)(2,1)}, bf16[2,512,6,128]{3,1,2,0:T(8,128)(2,1)S(1)}, u32[]{:S(2)}, u32[]{:S(2)}) collective-permute-start(bf16[2,512,6,128]{3,1,2,0:T(8,128)(2,1)} %pad_maximum_fusion), channel_id=1, source_target_pairs={{0,8},{2,10},{4,12},{6,14},{8,16},{10,18},{12,20},{14,22},{16,24},... | collective-permute-start | bytes 4718600 | tf_op jit(solution)/shard_map/ppermute | solution.py:16
  78.6 72.6 %copy-start.9 = (pred[64,8,4,128]{3,1,2,0:T(8,128)(4,1)S(1)}, pred[64,8,4,128]{3,1,2,0:T(8,128)(4,1)}, u32[]{:S(2)}) copy-start(pred[64,8,4,128]{3,1,2,0:T(8,128)(4,1)} %copy.204) | copy-start | bytes 786436
  153.6 6.1 %copy-start.3 = (pred[64,8,4,128]{3,1,2,0:T(8,128)(4,1)S(1)}, pred[64,8,4,128]{3,1,2,0:T(8,128)(4,1)}, u32[]{:S(2)}) copy-start(pred[64,8,4,128]{3,1,2,0:T(8,128)(4,1)} %copy.201) | copy-start | bytes 786436
  155.9 6.1 %copy-start.15 = (bf16[2,512,6,128]{3,1,2,0:T(8,128)(2,1)}, bf16[2,512,6,128]{3,1,2,0:T(8,128)(2,1)S(1)}, u32[]{:S(2)}) copy-start(bf16[2,512,6,128]{3,1,2,0:T(8,128)(2,1)S(1)} %collective-permute-done.4) | copy-start | bytes 4718596
  167.9 10.0 %slice-start = ((s8[6291456]{0:T(1024)(128)(4,1)}), s8[4194304]{0:T(1024)(128)(4,1)S(1)}, s32[]{:S(2)}) async-start(s8[6291456]{0:T(1024)(128)(4,1)} %bitcast.359), calls=%async_computation.5 | async-start | bytes 8388608
  171.1 6.7 %slice-start.1 = ((s8[6291456]{0:T(1024)(128)(4,1)}), s8[2097152]{0:T(1024)(128)(4,1)S(1)}, s32[]{:S(2)}) async-start(s8[6291456]{0:T(1024)(128)(4,1)} %bitcast.359), calls=%async_computation.6 | async-start | bytes 4194304
  176.4 5.8 %copy-start.23 = (f32[6,512]{1,0:T(8,128)S(1)}, f32[6,512]{1,0:T(8,128)}, u32[]{:S(2)}) copy-start(f32[6,512]{1,0:T(8,128)} %copy-done.22) | copy-start | bytes 36868
  195.0 25.1 %copy-start.33 = (bf16[256,1536]{1,0:T(8,128)(2,1)S(1)}, bf16[256,1536]{1,0:T(8,128)(2,1)}, u32[]{:S(2)}) copy-start(bf16[256,1536]{1,0:T(8,128)(2,1)} %param.11) | copy-start | bytes 2359300
  203.1 16.4 %all-to-all-start.3 = ((bf16[512,6,128]{2,1,0:T(8,128)(2,1)}), bf16[512,6,128]{2,1,0:T(8,128)(2,1)S(1)}, u32[]{:S(2)}, u32[]{:S(2)}) async-start(bf16[512,6,128]{2,1,0:T(8,128)(2,1)} %copy.152), calls=%async_computation.3 | async-start | bytes 2097152 | tf_op jit(solution)/shard_map/all_to_all | solution.py:73
  (25 other events, 90.1 us)
Sparse Core Ops, SparseCore 0:
  43.1 64.1 all-gather.1
where the time goes:
time: 233 us; the launch traced here: 232 us
  waiting for transfers between devices  98.6 us (42%)
  matrix products  48.2 us (21%)
  starting transfers between devices  33.1 us (14%)
  other arithmetic  19.3 us (8%)
  local copies, waits for them, and re-layouts  17.6 us (8%)
  between operations  14.8 us (6%)
    ppermute x6, waiting for transfers between devices, from_behind(): return lax.ppermute(shard, axis, pairs)  68 us
    dot_general x7, matrix products, fold_slot(): jnp.einsum('hqk,khd->qhd', exp_scores.astype(jnp.bfloat16), key_values[1]...  26.3 us
    ppermute x6, starting transfers between devices, from_behind(): return lax.ppermute(shard, axis, pairs)  18.8 us
    dot_general x7, matrix products, fold_slot(): jnp.einsum('qhd,khd->hqk', queries, key_values[0], preferred_element_type...  17.3 us
    reduce_sum x4, other arithmetic, fold_slot(): run_total = run_total * rescale + jnp.sum(exp_scores, axis=2)  15.1 us
    all_to_all x1, waiting for transfers between devices, body(): lax.all_to_all(attention, 'head', split_axis=0, concat_axis=1, tiled=True)  12.1 us
    unnamed x86, local copies, waits for them, and re-layouts  11.9 us
    all_to_all x1, waiting for transfers between devices, body(): lax.all_to_all(shaped[2], 'head', split_axis=1, concat_axis=0, tiled=True)  9 us
  transfers between devices with their start and end apart: 11, of which 4 were waited for; matrix products, arithmetic and copies ran while one was open for 34% of the time, Pallas kernels for 0%

commit v1 on v0

v1 whole, which is shorter than its diff:
```python
import functools
import math

import jax
import jax.numpy as jnp
from jax import lax
from jax.experimental import pallas as pl
from jax.experimental.pallas import tpu as pltpu
from jax.sharding import PartitionSpec as P

HEAD_DIM = 128
BLOCK = 128
OFFSETS = (0, -1, 1, -2, 2, -4, 4)
MESH = pl.DeviceIdType.MESH
MASKED = -1e30
EXP_SCALE = math.log2(math.e) / math.sqrt(HEAD_DIM)


def kernel(
    n, groups, q_any, k_any, v_any, res_any, levels, gate_any, mask, w_any, out,
    kv, qb, s_ref, mx_ref, tot_ref, acc_ref, att, att_tx, w, res, gate, bias,
    loc, a2a_tx, a2a_rx, tx, rx, w_tx, w_rx, w_stx, w_srx, att_ts, att_rs, misc,
):
    f = lax.axis_index("ctx")
    x = lax.axis_index("head")
    core = lax.rem(f, 2)
    y = lax.rem(f // 2, 2)
    rows = q_any.shape[0]
    heads = kv.shape[1]
    slots = kv.shape[0]
    frame = kv.shape[3]
    blocks = frame // BLOCK
    depth = w_any.shape[0]
    half = depth // 2
    piece = half // heads
    sib = f + 1 - 2 * core
    pair = f + 2 - 4 * y
    far = f + 4 - 8 * y
    has_up = f + 4 < n
    has_down = f >= 4
    relays = jnp.logical_or(jnp.logical_and(y == 0, has_up), jnp.logical_and(y == 1, has_down))
    passes_on = jnp.logical_or(
        jnp.logical_and(core == 1, f >= 2), jnp.logical_and(core == 0, f + 2 < n)
    )

    def valid(s):
        return jnp.logical_and(f + OFFSETS[s] >= 0, f + OFFSETS[s] < n)

    def peer(j):
        return lax.rem(x + j, groups)

    def source(j):
        return lax.rem(x + groups - j, groups)

    def remote(src, dst, send, recv, dev):
        return pltpu.make_async_remote_copy(
            src_ref=src, dst_ref=dst, send_sem=send, recv_sem=recv,
            device_id=dev, device_id_type=MESH,
        )

    def cols(group, h):
        return pl.ds(pl.multiple_of((group * heads + h) * HEAD_DIM, HEAD_DIM), HEAD_DIM)

    def own_rows(group):
        return pl.ds(pl.multiple_of(group * rows, rows), rows)

    operands = (k_any, v_any, q_any)

    def landing(kind, h, group):
        if kind == 2:
            return qb.at[h, own_rows(group), :]
        return kv.at[0, h, kind, own_rows(group), :]

    def local_in(kind, h):
        return pltpu.make_async_copy(
            operands[kind].at[:, cols(x, h)], landing(kind, h, x), loc.at[kind, h]
        )

    def swap(kind, h, j, group):
        return remote(
            operands[kind].at[:, cols(peer(j), h)], landing(kind, h, group),
            a2a_tx.at[j - 1, kind, h], a2a_rx.at[j - 1, kind, h], (f, peer(j)),
        )

    def direct(which, kind, h):
        slot, dev = ((5, f + 4), (6, f - 4), (3 + y, pair), (1 + core, sib))[which]
        return remote(
            kv.at[0, h, kind], kv.at[slot, h, kind],
            tx.at[which, kind, h], rx.at[slot, kind, h], (dev, x),
        )

    def relay(kind, h):
        if kind == 0:
            src, slot, dev = 4 - y, 3 + y, far
        else:
            src, slot, dev = 6 - y, 4 - y, pair
        return remote(
            kv.at[src, h, kind], kv.at[slot, h, kind],
            tx.at[4, kind, h], rx.at[slot, kind, h], (dev, x),
        )

    def pass_on(kind, h):
        return remote(
            kv.at[4 - core, h, kind], kv.at[2 - core, h, kind],
            tx.at[5, kind, h], rx.at[2 - core, kind, h], (sib, x),
        )

    def wait_slot(slot, kind, h):
        remote(
            kv.at[0, h, kind], kv.at[slot, h, kind],
            tx.at[0, kind, h], rx.at[slot, kind, h], (sib, x),
        ).wait_recv()

    def weight_rows(group, c, t):
        return pl.ds(pl.multiple_of(group * depth + c * half + t * piece, piece), piece)

    def weight_send(t, j, group):
        return remote(
            w_any.at[pl.ds(pl.multiple_of(core * half + t * piece, piece), piece), :],
            w.at[weight_rows(group, core, t), :],
            w_tx.at[j - 1, t], w_rx.at[j - 1, t], (f, peer(j)),
        )

    def weight_share(t, j, c):
        return remote(
            w.at[weight_rows(source(j), core, t), :], w.at[weight_rows(source(j), c, t), :],
            w_stx.at[j - 1, t], w_srx.at[j - 1, t], (sib, x),
        )

    def att_send(h, j, group):
        return remote(
            att_tx.at[j - 1, h], att.at[:, cols(group, h)],
            att_ts.at[j - 1, h], att_rs.at[j - 1, h], (f, peer(j)),
        )

    others = (
        pltpu.make_async_copy(res_any, res, misc.at[0]),
        pltpu.make_async_copy(gate_any, gate, misc.at[1]),
        pltpu.make_async_copy(
            w_any, w.at[pl.ds(pl.multiple_of(x * depth, depth), depth), :], misc.at[2]
        ),
    )

    barrier = pltpu.get_barrier_semaphore()

    def greet(dev):
        pl.semaphore_signal(barrier, inc=1, device_id=dev, device_id_type=MESH)

    greet((sib, x))
    greet((pair, x))
    for j in range(1, groups):
        greet((f, peer(j)))
    pl.when(has_up)(lambda: greet((f + 4, x)))
    pl.when(has_down)(lambda: greet((f - 4, x)))

    @pl.loop(0, heads)
    def _(h):
        for kind in range(3):
            local_in(kind, h).start()

    pl.semaphore_wait(barrier, 1 + groups + has_up.astype(jnp.int32) + has_down.astype(jnp.int32))

    @pl.loop(0, heads)
    def _(h):
        for j in range(1, groups):
            for kind in range(3):
                swap(kind, h, j, x).start()

    for copy in others:
        copy.start()

    for s in range(slots):
        for a in range(blocks):
            for b in range(blocks):
                kept = mask[0, s, a, b] > 0
                bias[s, a : a + 1, b * BLOCK : (b + 1) * BLOCK] = jnp.full(
                    (1, BLOCK), jnp.where(kept, 0.0, MASKED), jnp.float32
                )

    for s in range(1, slots):

        @pl.when(jnp.logical_not(valid(s)))
        def _():
            @pl.loop(0, heads)
            def _(h):
                for kind in range(2):
                    kv[s, h, kind] = jnp.zeros((frame, HEAD_DIM), kv.dtype)

    def send_direct(h):
        for kind in range(2):
            local_in(kind, h).wait()
            for j in range(1, groups):
                swap(kind, h, j, source(j)).wait_recv()

        @pl.when(has_up)
        def _():
            for kind in range(2):
                direct(0, kind, h).start()

        @pl.when(has_down)
        def _():
            for kind in range(2):
                direct(1, kind, h).start()

        for which in (2, 3):
            for kind in range(2):
                direct(which, kind, h).start()

    def send_relay(h):
        @pl.when(relays)
        def _():
            wait_slot(4 - y, 0, h)
            relay(0, h).start()
            wait_slot(6 - y, 1, h)
            relay(1, h).start()

    def send_on(h):
        @pl.when(passes_on)
        def _():
            pl.when(jnp.logical_not(jnp.logical_and(relays, core == y)))(
                lambda: wait_slot(4 - core, 0, h)
            )
            pass_on(0, h).start()
            wait_slot(4 - core, 1, h)
            pass_on(1, h).start()

    def attend(h):
        local_in(2, h).wait()
        for j in range(1, groups):
            swap(2, h, j, source(j)).wait_recv()
        for s in range(1, slots):
            for kind in range(2):
                known = jnp.logical_and(relays, (4 - y if kind == 0 else 6 - y) == s)
                passed = jnp.logical_and(passes_on, 4 - core == s)
                due = jnp.logical_and(valid(s), jnp.logical_not(jnp.logical_or(known, passed)))
                pl.when(due)(functools.partial(wait_slot, s, kind, h))

        mx_ref[...] = jnp.full_like(mx_ref, MASKED)
        tot_ref[...] = jnp.zeros_like(tot_ref)
        acc_ref[...] = jnp.zeros_like(acc_ref)

        @pl.loop(0, slots)
        def _(s):
            for a in range(blocks):
                r = slice(a * BLOCK, (a + 1) * BLOCK)
                scores = lax.dot_general(
                    qb[h, r], kv[s, h, 0], (((1,), (1,)), ((), ())),
                    preferred_element_type=jnp.float32,
                ) + bias[s, a : a + 1, :]
                s_ref[s, r, :] = scores
                top = mx_ref[r]
                for b in range(blocks):
                    top = jnp.maximum(top, scores[:, b * BLOCK : (b + 1) * BLOCK])
                mx_ref[r] = top

        mx_ref[...] = jnp.broadcast_to(jnp.max(mx_ref[...], axis=1, keepdims=True), mx_ref.shape)

        @pl.loop(0, slots)
        def _(s):
            for a in range(blocks):
                r = slice(a * BLOCK, (a + 1) * BLOCK)
                top = mx_ref[r]
                total = tot_ref[r]
                parts = []
                for b in range(blocks):
                    e = jnp.exp2((s_ref[s, r, b * BLOCK : (b + 1) * BLOCK] - top) * EXP_SCALE)
                    total = total + e
                    parts.append(e.astype(jnp.bfloat16))
                tot_ref[r] = total
                acc_ref[r] += jnp.dot(
                    jnp.concatenate(parts, axis=1), kv[s, h, 1],
                    preferred_element_type=jnp.float32,
                )

        def share(group):
            r = own_rows(group)
            total = jnp.sum(tot_ref[r, :], axis=1, keepdims=True)
            return (acc_ref[r, :] / total).astype(jnp.bfloat16)

        for j in range(1, groups):
            att_tx[j - 1, h] = share(peer(j))
            att_send(h, j, x).start()
        att[:, cols(x, h)] = share(x)

    @pl.loop(0, heads + 3)
    def _(t):
        @pl.when(t < heads)
        def _():
            send_direct(t)
            for j in range(1, groups):
                weight_send(t, j, x).start()

        pl.when(jnp.logical_and(t >= 1, t < heads + 1))(lambda: send_relay(t - 1))
        pl.when(t >= 3)(lambda: attend(t - 3))

        @pl.when(jnp.logical_and(t >= 2, t < heads + 2))
        def _():
            send_on(t - 2)
            for j in range(1, groups):
                weight_send(t - 2, j, source(j)).wait_recv()
                weight_share(t - 2, j, core).start()

    for copy in others:
        copy.wait()

    @pl.loop(0, heads)
    def _(h):
        for j in range(1, groups):
            weight_share(h, j, 1 - core).wait_recv()
            att_send(h, j, source(j)).wait_recv()

    level = levels[0]
    gate_row = gate[pl.ds(level, 1), :]
    width = 2 * HEAD_DIM
    for at in range(0, out.shape[1], width):
        c = slice(at, at + width)
        projected = jnp.dot(att[...], w[:, c], preferred_element_type=jnp.float32)
        out[:, c] = (res[:, c].astype(jnp.float32) + gate_row[:, c] * projected).astype(out.dtype)

    @pl.loop(0, heads)
    def _(h):
        for j in range(1, groups):
            for kind in range(3):
                swap(kind, h, j, x).wait_send()
            weight_send(h, j, x).wait_send()
            weight_share(h, j, core).wait_send()
            att_send(h, j, x).wait_send()
        for kind in range(2):
            for which in (2, 3):
                direct(which, kind, h).wait_send()
            pl.when(has_up)(lambda: direct(0, kind, h).wait_send())
            pl.when(has_down)(lambda: direct(1, kind, h).wait_send())
            pl.when(relays)(lambda: relay(kind, h).wait_send())
            pl.when(passes_on)(lambda: pass_on(kind, h).wait_send())


def body(n, groups, *operands):
    query_rows, gate_table, block_mask, out_weight = (operands[i] for i in (0, 5, 6, 7))
    rows, width = query_rows.shape
    slots, blocks = block_mask.shape[1], block_mask.shape[2]
    frame = rows * groups
    heads = width // HEAD_DIM // groups
    any_space = pl.BlockSpec(memory_space=pl.ANY)
    smem = pl.BlockSpec(memory_space=pltpu.SMEM)
    bf16, f32 = jnp.bfloat16, jnp.float32
    dma = pltpu.SemaphoreType.DMA
    pairs = frame * slots * frame * heads
    return pl.pallas_call(
        functools.partial(kernel, n, groups),
        out_shape=jax.ShapeDtypeStruct((rows, width), bf16),
        in_specs=[any_space] * 4 + [smem, any_space, smem, any_space],
        out_specs=pl.BlockSpec(memory_space=pltpu.VMEM),
        scratch_shapes=[
            pltpu.VMEM((slots, heads, 2, frame, HEAD_DIM), bf16),
            pltpu.VMEM((heads, frame, HEAD_DIM), bf16),
            pltpu.VMEM((slots, frame, frame), f32),
            pltpu.VMEM((frame, HEAD_DIM), f32),
            pltpu.VMEM((frame, HEAD_DIM), f32),
            pltpu.VMEM((frame, HEAD_DIM), f32),
            pltpu.VMEM((rows, width), bf16),
            pltpu.VMEM((groups - 1, heads, rows, HEAD_DIM), bf16),
            pltpu.VMEM((width, width), bf16),
            pltpu.VMEM((rows, width), bf16),
            pltpu.VMEM(gate_table.shape, f32),
            pltpu.VMEM((slots, blocks, frame), f32),
            dma((3, heads)),
            dma((groups - 1, 3, heads)),
            dma((groups - 1, 3, heads)),
            dma((6, 2, heads)),
            dma((slots, 2, heads)),
            dma((groups - 1, heads)),
            dma((groups - 1, heads)),
            dma((groups - 1, heads)),
            dma((groups - 1, heads)),
            dma((groups - 1, heads)),
            dma((groups - 1, heads)),
            dma((3,)),
        ],
        compiler_params=pltpu.CompilerParams(
            collective_id=0, has_side_effects=True, vmem_limit_bytes=48 * 1024 * 1024
        ),
        cost_estimate=pl.CostEstimate(
            flops=4 * pairs * HEAD_DIM + 2 * rows * width * width,
            bytes_accessed=2 * (5 * rows * width + width * width // groups),
            transcendentals=pairs,
        ),
    )(*operands)


def solution(mesh):
    return jax.shard_map(
        functools.partial(body, mesh.shape["ctx"], mesh.shape["head"]),
        mesh=mesh,
        in_specs=(
            P(("ctx", "head"), None),
            P(("ctx", "head"), None),
            P(("ctx", "head"), None),
            P(("ctx", "head"), None),
            P("ctx"),
            P(),
            P("ctx", None, None, None),
            P("head", None),
        ),
        out_specs=P(("ctx", "head"), None),
        check_vma=False,
    )
```

time: 233 us -> 89.3 us (0.38)
  waiting for transfers between devices: 98.6 us -> 0 us
  Pallas kernels: 0 us -> 80.4 us
  matrix products: 48.2 us -> 0 us
  starting transfers between devices: 33.1 us -> 0 us
  other arithmetic: 19.3 us -> 0 us
  between operations: 14.8 us -> 0.67 us
  local copies, waits for them, and re-layouts: 17.6 us -> 7.19 us
    pallas_call x0 -> x1, Pallas kernels: none -> 80.4 us  [body(): pl.pallas_call(functools.partial(kernel, n, groups), out_shape=jax.ShapeD...]
    ppermute x6 -> x0, waiting for transfers between devices: 68 us -> none  [from_behind(): return lax.ppermute(shard, axis, pairs)]
    dot_general x15 -> x0, matrix products: 48.2 us -> none  [the longest x7 26.3 us: fold_slot(): jnp.einsum('hqk,khd->qhd', exp_scores.astype(jnp.bfloat16), key_values[1]...]
    all_to_all x4 -> x0, waiting for transfers between devices: 29.9 us -> none  [the longest x1 12.1 us: body(): lax.all_to_all(attention, 'head', split_axis=0, concat_axis=1, tiled=True)]
    ppermute x6 -> x0, starting transfers between devices: 18.8 us -> none  [from_behind(): return lax.ppermute(shard, axis, pairs)]
    reduce_sum x4 -> x0, other arithmetic: 15.1 us -> none  [fold_slot(): run_total = run_total * rescale + jnp.sum(exp_scores, axis=2)]
    all_to_all x4 -> x0, starting transfers between devices: 14.2 us -> none  [the longest x1 3.58 us: body(): lax.all_to_all(attention, 'head', split_axis=0, concat_axis=1, tiled=True)]
    unnamed x86 -> x12, local copies, waits for them, and re-layouts: 11.9 us -> 7.19 us
  transfers between devices with their start and end apart: 11 -> 0, of which waited for: 4 -> 0; matrix products, arithmetic and copies ran while one was open for 34% -> 0% of each run, Pallas kernels for 0% -> 0%
where the time goes in v1:
time: 89.3 us; the launch traced here: 88.2 us
  Pallas kernels  80.4 us (90%)
  local copies, waits for them, and re-layouts  7.19 us (8%)
    pallas_call x1, Pallas kernels, body(): pl.pallas_call(functools.partial(kernel, n, groups), out_shape=jax.ShapeD...  80.4 us
    unnamed x12, local copies, waits for them, and re-layouts  7.19 us

profile of v1, /device:TPU:20, one launch (start us, length us, event | category | flops | bytes accessed | tf_op | source)
XLA Modules:
  0.0 88.2 jit_solution(12063129937754109304)
XLA Ops:
  0.7 0.8 copy.9.mask
  1.5 0.0 copy-start
  1.5 1.1 %copy-done = bf16[256,1536]{1,0:T(8,128)(2,1)S(1)} copy-done((bf16[256,1536]{1,0:T(8,128)(2,1)S(1)}, bf16[256,1536]{1,0:T(8,128)(2,1)}, u32[]{:S(2)}) %copy-start) | copy-done | bytes 786456
  2.6 0.0 copy-start.1
  2.6 1.1 %copy-done.1 = bf16[256,1536]{1,0:T(8,128)(2,1)S(1)} copy-done((bf16[256,1536]{1,0:T(8,128)(2,1)S(1)}, bf16[256,1536]{1,0:T(8,128)(2,1)}, u32[]{:S(2)}) %copy-start.1) | copy-done | bytes 786456
  3.7 0.0 copy-start.2
  3.7 1.1 %copy-done.2 = bf16[256,1536]{1,0:T(8,128)(2,1)S(1)} copy-done((bf16[256,1536]{1,0:T(8,128)(2,1)S(1)}, bf16[256,1536]{1,0:T(8,128)(2,1)}, u32[]{:S(2)}) %copy-start.2) | copy-done | bytes 786456
  4.9 0.0 copy-start.3
  4.9 1.1 %copy-done.3 = bf16[256,1536]{1,0:T(8,128)(2,1)S(1)} copy-done((bf16[256,1536]{1,0:T(8,128)(2,1)S(1)}, bf16[256,1536]{1,0:T(8,128)(2,1)}, u32[]{:S(2)}) %copy-start.3) | copy-done | bytes 786456
  6.0 0.0 copy-start.4
  6.0 1.0 %copy-done.4 = f32[50,1536]{1,0:T(8,128)S(1)} copy-done((f32[50,1536]{1,0:T(8,128)S(1)}, f32[50,1536]{1,0:T(8,128)}, u32[]{:S(2)}) %copy-start.4) | copy-done | bytes 307224
  7.0 80.4 %shard_map.82 = bf16[256,1536]{1,0:T(8,128)(2,1)S(1)} custom-call(bf16[256,1536]{1,0:T(8,128)(2,1)S(1)} %copy-done, bf16[256,1536]{1,0:T(8,128)(2,1)S(1)} %copy-done.1, bf16[256,1536]{1,0:T(8,128)(2,1)S(1)} %copy-done.2, bf16[256,1536]{1,0:T(8,128)(2,1)S(1)} %copy-done.3, s32[1]{0:T(128)S(6)} %copy.11.levels, f32[50,1536]{1,0:T(8,128)S(1)} %copy-done.4, ...), custom_call_target="tpu_custom_call" | custom-call | flops 6845104128 | bytes 6291456 | tf_op jit(solution)/shard_map/pallas_call | solution.py:348
  87.3 0.9 copy.12
Async XLA Ops:
  1.5 1.1 %copy-start = (bf16[256,1536]{1,0:T(8,128)(2,1)S(1)}, bf16[256,1536]{1,0:T(8,128)(2,1)}, u32[]{:S(2)}) copy-start(bf16[256,1536]{1,0:T(8,128)(2,1)} %q_any.1) | copy-start | bytes 2359300
  2.6 1.1 %copy-start.1 = (bf16[256,1536]{1,0:T(8,128)(2,1)S(1)}, bf16[256,1536]{1,0:T(8,128)(2,1)}, u32[]{:S(2)}) copy-start(bf16[256,1536]{1,0:T(8,128)(2,1)} %k_any.1) | copy-start | bytes 2359300
  3.7 1.1 %copy-start.2 = (bf16[256,1536]{1,0:T(8,128)(2,1)S(1)}, bf16[256,1536]{1,0:T(8,128)(2,1)}, u32[]{:S(2)}) copy-start(bf16[256,1536]{1,0:T(8,128)(2,1)} %v_any.1) | copy-start | bytes 2359300
  4.9 1.1 %copy-start.3 = (bf16[256,1536]{1,0:T(8,128)(2,1)S(1)}, bf16[256,1536]{1,0:T(8,128)(2,1)}, u32[]{:S(2)}) copy-start(bf16[256,1536]{1,0:T(8,128)(2,1)} %res_any.1) | copy-start | bytes 2359300
  6.0 1.0 %copy-start.4 = (f32[50,1536]{1,0:T(8,128)S(1)}, f32[50,1536]{1,0:T(8,128)}, u32[]{:S(2)}) copy-start(f32[50,1536]{1,0:T(8,128)} %gate_any.1) | copy-start | bytes 921604

commit v2 on v1

--- a/solution.py
+++ b/solution.py
@@ -13,12 +13,13 @@
 OFFSETS = (0, -1, 1, -2, 2, -4, 4)
 MESH = pl.DeviceIdType.MESH
 MASKED = -1e30
+AHEAD = 2
 EXP_SCALE = math.log2(math.e) / math.sqrt(HEAD_DIM)
 
 
 def kernel(
-    n, groups, q_any, k_any, v_any, res_any, levels, gate_any, mask, w_any, out,
-    kv, qb, s_ref, mx_ref, tot_ref, acc_ref, att, att_tx, w, res, gate, bias,
+    n, groups, q_any, k_any, v_any, res_any, levels, gate_any, mask_any, w_any, out,
+    kv, qb, s_ref, mx_ref, top_ref, tot_ref, acc_ref, att, att_tx, w, res, gate, mask, bias,
     loc, a2a_tx, a2a_rx, tx, rx, w_tx, w_rx, w_stx, w_srx, att_ts, att_rs, misc,
 ):
     f = lax.axis_index("ctx")
@@ -133,6 +134,8 @@
             att_ts.at[j - 1, h], att_rs.at[j - 1, h], (f, peer(j)),
         )
 
+    mask_in = pltpu.make_async_copy(mask_any, mask, misc.at[3])
+    mask_in.start()
     others = (
         pltpu.make_async_copy(res_any, res, misc.at[0]),
         pltpu.make_async_copy(gate_any, gate, misc.at[1]),
@@ -160,22 +163,24 @@
 
     pl.semaphore_wait(barrier, 1 + groups + has_up.astype(jnp.int32) + has_down.astype(jnp.int32))
 
-    @pl.loop(0, heads)
-    def _(h):
+    def send_swap(kinds, h):
         for j in range(1, groups):
-            for kind in range(3):
+            for kind in kinds:
                 swap(kind, h, j, x).start()
+
+    for h in range(min(AHEAD, heads)):
+        send_swap((0, 1), h)
 
     for copy in others:
         copy.start()
 
+    mask_in.wait()
     for s in range(slots):
-        for a in range(blocks):
-            for b in range(blocks):
-                kept = mask[0, s, a, b] > 0
-                bias[s, a : a + 1, b * BLOCK : (b + 1) * BLOCK] = jnp.full(
-                    (1, BLOCK), jnp.where(kept, 0.0, MASKED), jnp.float32
-                )
+        off = jnp.where(mask[0, s] > 0, 0.0, MASKED)
+        for b in range(blocks):
+            bias[s, :, b * BLOCK : (b + 1) * BLOCK] = jnp.broadcast_to(
+                off[:, b : b + 1], (blocks, BLOCK)
+            )
 
     for s in range(1, slots):
 
@@ -217,65 +222,96 @@
     def send_on(h):
         @pl.when(passes_on)
         def _():
-            pl.when(jnp.logical_not(jnp.logical_and(relays, core == y)))(
-                lambda: wait_slot(4 - core, 0, h)
-            )
-            pass_on(0, h).start()
-            wait_slot(4 - core, 1, h)
-            pass_on(1, h).start()
-
-    def attend(h):
-        local_in(2, h).wait()
-        for j in range(1, groups):
-            swap(2, h, j, source(j)).wait_recv()
+            for kind in range(2):
+                pl.when(core != y)(functools.partial(wait_slot, 4 - core, kind, h))
+                pass_on(kind, h).start()
+
+    def early(i):
+        picks = (0, 5, 6, 4 - y, 2 - core)
+        slot = picks[-1]
+        for k in range(len(picks) - 1):
+            slot = jnp.where(i == k, picks[k], slot)
+        return slot
+
+    def late(i):
+        return jnp.where(i == 0, 3 + y, 1 + core)
+
+    def wait_slots(h, now):
         for s in range(1, slots):
+            is_late = jnp.logical_or(3 + y == s, 1 + core == s)
+            mine = is_late if now == "late" else jnp.logical_not(is_late)
             for kind in range(2):
                 known = jnp.logical_and(relays, (4 - y if kind == 0 else 6 - y) == s)
-                passed = jnp.logical_and(passes_on, 4 - core == s)
+                passed = jnp.logical_and(jnp.logical_and(passes_on, core != y), 3 + y == s)
                 due = jnp.logical_and(valid(s), jnp.logical_not(jnp.logical_or(known, passed)))
-                pl.when(due)(functools.partial(wait_slot, s, kind, h))
-
-        mx_ref[...] = jnp.full_like(mx_ref, MASKED)
-        tot_ref[...] = jnp.zeros_like(tot_ref)
-        acc_ref[...] = jnp.zeros_like(acc_ref)
-
-        @pl.loop(0, slots)
-        def _(s):
+                pl.when(jnp.logical_and(due, mine))(functools.partial(wait_slot, s, kind, h))
+
+    def fold(h, count, pick, first):
+        state = lax.rem(h, 2)
+        if first:
+            mx_ref[...] = jnp.full_like(mx_ref, MASKED)
+        else:
+            mx_ref[...] = top_ref[state]
+
+        @pl.loop(0, count)
+        def _(i):
+            s = pick(i)
             for a in range(blocks):
                 r = slice(a * BLOCK, (a + 1) * BLOCK)
                 scores = lax.dot_general(
                     qb[h, r], kv[s, h, 0], (((1,), (1,)), ((), ())),
                     preferred_element_type=jnp.float32,
                 ) + bias[s, a : a + 1, :]
-                s_ref[s, r, :] = scores
+                s_ref[i, r, :] = scores
                 top = mx_ref[r]
                 for b in range(blocks):
                     top = jnp.maximum(top, scores[:, b * BLOCK : (b + 1) * BLOCK])
                 mx_ref[r] = top
 
-        mx_ref[...] = jnp.broadcast_to(jnp.max(mx_ref[...], axis=1, keepdims=True), mx_ref.shape)
-
-        @pl.loop(0, slots)
-        def _(s):
+        new_top = jnp.broadcast_to(jnp.max(mx_ref[...], axis=1, keepdims=True), mx_ref.shape)
+        if first:
+            tot_ref[state] = jnp.zeros(mx_ref.shape, jnp.float32)
+            acc_ref[state] = jnp.zeros(mx_ref.shape, jnp.float32)
+        else:
+            fade = jnp.exp2((top_ref[state] - new_top) * EXP_SCALE)
+            tot_ref[state] = tot_ref[state] * fade
+            acc_ref[state] = acc_ref[state] * fade
+        top_ref[state] = new_top
+
+        @pl.loop(0, count)
+        def _(i):
+            s = pick(i)
             for a in range(blocks):
                 r = slice(a * BLOCK, (a + 1) * BLOCK)
-                top = mx_ref[r]
-                total = tot_ref[r]
+                top = top_ref[state, r]
+                total = tot_ref[state, r]
                 parts = []
                 for b in range(blocks):
-                    e = jnp.exp2((s_ref[s, r, b * BLOCK : (b + 1) * BLOCK] - top) * EXP_SCALE)
+                    e = jnp.exp2((s_ref[i, r, b * BLOCK : (b + 1) * BLOCK] - top) * EXP_SCALE)
                     total = total + e
                     parts.append(e.astype(jnp.bfloat16))
-                tot_ref[r] = total
-                acc_ref[r] += jnp.dot(
+                tot_ref[state, r] = total
+                acc_ref[state, r] += jnp.dot(
                     jnp.concatenate(parts, axis=1), kv[s, h, 1],
                     preferred_element_type=jnp.float32,
                 )
 
+    def attend_early(h):
+        local_in(2, h).wait()
+        for j in range(1, groups):
+            swap(2, h, j, source(j)).wait_recv()
+        wait_slots(h, "early")
+        fold(h, slots - 2, early, True)
+
+    def attend_late(h):
+        wait_slots(h, "late")
+        fold(h, 2, late, False)
+        state = lax.rem(h, 2)
+
         def share(group):
             r = own_rows(group)
-            total = jnp.sum(tot_ref[r, :], axis=1, keepdims=True)
-            return (acc_ref[r, :] / total).astype(jnp.bfloat16)
+            total = jnp.sum(tot_ref[state, r, :], axis=1, keepdims=True)
+            return (acc_ref[state, r, :] / total).astype(jnp.bfloat16)
 
         for j in range(1, groups):
             att_tx[j - 1, h] = share(peer(j))
@@ -286,12 +322,14 @@
     def _(t):
         @pl.when(t < heads)
         def _():
+            pl.when(t + AHEAD < heads)(lambda: send_swap((0, 1), t + AHEAD))
+            send_swap((2,), t)
             send_direct(t)
             for j in range(1, groups):
                 weight_send(t, j, x).start()
 
         pl.when(jnp.logical_and(t >= 1, t < heads + 1))(lambda: send_relay(t - 1))
-        pl.when(t >= 3)(lambda: attend(t - 3))
+        pl.when(jnp.logical_and(t >= 2, t < heads + 2))(lambda: attend_early(t - 2))
 
         @pl.when(jnp.logical_and(t >= 2, t < heads + 2))
         def _():
@@ -299,6 +337,8 @@
             for j in range(1, groups):
                 weight_send(t - 2, j, source(j)).wait_recv()
                 weight_share(t - 2, j, core).start()
+
+        pl.when(jnp.logical_and(t >= 3, t < heads + 3))(lambda: attend_late(t - 3))
 
     for copy in others:
         copy.wait()
@@ -340,7 +380,7 @@
     slots, blocks = block_mask.shape[1], block_mask.shape[2]
     frame = rows * groups
     heads = width // HEAD_DIM // groups
-    any_space = pl.BlockSpec(memory_space=pl.ANY)
+    any_space = pl.BlockSpec(memory_space=pltpu.HBM)
     smem = pl.BlockSpec(memory_space=pltpu.SMEM)
     bf16, f32 = jnp.bfloat16, jnp.float32
     dma = pltpu.SemaphoreType.DMA
@@ -348,20 +388,22 @@
     return pl.pallas_call(
         functools.partial(kernel, n, groups),
         out_shape=jax.ShapeDtypeStruct((rows, width), bf16),
-        in_specs=[any_space] * 4 + [smem, any_space, smem, any_space],
+        in_specs=[any_space] * 4 + [smem] + [any_space] * 3,
         out_specs=pl.BlockSpec(memory_space=pltpu.VMEM),
         scratch_shapes=[
             pltpu.VMEM((slots, heads, 2, frame, HEAD_DIM), bf16),
             pltpu.VMEM((heads, frame, HEAD_DIM), bf16),
-            pltpu.VMEM((slots, frame, frame), f32),
+            pltpu.VMEM((slots - 2, frame, frame), f32),
             pltpu.VMEM((frame, HEAD_DIM), f32),
-            pltpu.VMEM((frame, HEAD_DIM), f32),
-            pltpu.VMEM((frame, HEAD_DIM), f32),
+            pltpu.VMEM((2, frame, HEAD_DIM), f32),
+            pltpu.VMEM((2, frame, HEAD_DIM), f32),
+            pltpu.VMEM((2, frame, HEAD_DIM), f32),
             pltpu.VMEM((rows, width), bf16),
             pltpu.VMEM((groups - 1, heads, rows, HEAD_DIM), bf16),
             pltpu.VMEM((width, width), bf16),
             pltpu.VMEM((rows, width), bf16),
             pltpu.VMEM(gate_table.shape, f32),
+            pltpu.VMEM(block_mask.shape, block_mask.dtype),
             pltpu.VMEM((slots, blocks, frame), f32),
             dma((3, heads)),
             dma((groups - 1, 3, heads)),
@@ -374,10 +416,10 @@
             dma((groups - 1, heads)),
             dma((groups - 1, heads)),
             dma((groups - 1, heads)),
-            dma((3,)),
+            dma((4,)),
         ],
         compiler_params=pltpu.CompilerParams(
-            collective_id=0, has_side_effects=True, vmem_limit_bytes=48 * 1024 * 1024
+            collective_id=0, has_side_effects=True, vmem_limit_bytes=60 * 1024 * 1024
         ),
         cost_estimate=pl.CostEstimate(
             flops=4 * pairs * HEAD_DIM + 2 * rows * width * width,

time: 89.3 us -> 77.3 us (0.87)
  Pallas kernels: 80.4 us -> 72.8 us
  local copies, waits for them, and re-layouts: 7.19 us -> 3.46 us
    pallas_call x1, Pallas kernels: 80.4 us -> 72.8 us  [body(): pl.pallas_call(functools.partial(kernel, n, groups), out_shape=jax.ShapeD...]
    unnamed x12 -> x2, local copies, waits for them, and re-layouts: 7.19 us -> 3.46 us
where the time goes in v2:
time: 77.3 us; the launch traced here: 76.9 us
  Pallas kernels  72.8 us (94%)
  local copies, waits for them, and re-layouts  3.46 us (4%)
    pallas_call x1, Pallas kernels, body(): pl.pallas_call(functools.partial(kernel, n, groups), out_shape=jax.ShapeD...  72.8 us
    unnamed x2, local copies, waits for them, and re-layouts  3.46 us

profile of v2, /device:TPU:20, one launch (start us, length us, event | category | flops | bytes accessed | tf_op | source)
XLA Modules:
  0.0 76.9 jit_solution(4429247579415875541)
XLA Ops:
  0.7 1.4 %copy.9.mask_any = s32[1,7,4,4]{3,2,1,0:T(4,128)} copy(s32[1,7,4,4]{1,3,2,0:T(4,128)} %param.14) | data formatting | bytes 896 | tf_op args[6]
  2.0 72.8 %shard_map.82 = bf16[256,1536]{1,0:T(8,128)(2,1)} custom-call(bf16[256,1536]{1,0:T(8,128)(2,1)} %q_any.1, bf16[256,1536]{1,0:T(8,128)(2,1)} %k_any.1, bf16[256,1536]{1,0:T(8,128)(2,1)} %v_any.1, bf16[256,1536]{1,0:T(8,128)(2,1)} %res_any.1, s32[1]{0:T(128)S(6)} %copy.11.levels, f32[50,1536]{1,0:T(8,128)} %gate_any.1, s32[1,7,4,4]{3,2,1,0:T(4,128)} %copy.9.mask_any, ...), custom_call_target="tpu_custom_call" | custom-call | flops 6845104128 | bytes 6291456 | tf_op jit(solution)/shard_map/pallas_call | solution.py:388
  74.9 2.1 %copy.12 = bf16[256,1536]{1,0:T(8,128)(2,1)} copy(bf16[256,1536]{1,0:T(8,128)(2,1)} %shard_map.82) | data formatting | bytes 1572864

commit v3 on v2

--- a/solution.py
+++ b/solution.py
@@ -253,7 +253,7 @@
         else:
             mx_ref[...] = top_ref[state]
 
-        @pl.loop(0, count)
+        @pl.loop(0, count, unroll=True)
         def _(i):
             s = pick(i)
             for a in range(blocks):
@@ -278,7 +278,7 @@
             acc_ref[state] = acc_ref[state] * fade
         top_ref[state] = new_top
 
-        @pl.loop(0, count)
+        @pl.loop(0, count, unroll=True)
         def _(i):
             s = pick(i)
             for a in range(blocks):
@@ -324,9 +324,9 @@
         def _():
             pl.when(t + AHEAD < heads)(lambda: send_swap((0, 1), t + AHEAD))
             send_swap((2,), t)
-            send_direct(t)
             for j in range(1, groups):
                 weight_send(t, j, x).start()
+            send_direct(t)
 
         pl.when(jnp.logical_and(t >= 1, t < heads + 1))(lambda: send_relay(t - 1))
         pl.when(jnp.logical_and(t >= 2, t < heads + 2))(lambda: attend_early(t - 2))

time: 77.3 us -> 74.8 us (0.968)
  Pallas kernels: 72.8 us -> 70.4 us
    pallas_call x1, Pallas kernels: 72.8 us -> 70.4 us  [body(): pl.pallas_call(functools.partial(kernel, n, groups), out_shape=jax.ShapeD...]
where the time goes in v3:
time: 74.8 us; the launch traced here: 74.5 us
  Pallas kernels  70.4 us (94%)
  local copies, waits for them, and re-layouts  3.46 us (5%)
    pallas_call x1, Pallas kernels, body(): pl.pallas_call(functools.partial(kernel, n, groups), out_shape=jax.ShapeD...  70.4 us
    unnamed x2, local copies, waits for them, and re-layouts  3.46 us

profile of v3, /device:TPU:20, one launch (start us, length us, event | category | flops | bytes accessed | tf_op | source)
XLA Modules:
  0.0 74.5 jit_solution(9882197688429871632)
XLA Ops:
  0.7 1.4 %copy.9.mask_any = s32[1,7,4,4]{3,2,1,0:T(4,128)} copy(s32[1,7,4,4]{1,3,2,0:T(4,128)} %param.14) | data formatting | bytes 896 | tf_op args[6]
  2.0 70.4 %shard_map.82 = bf16[256,1536]{1,0:T(8,128)(2,1)} custom-call(bf16[256,1536]{1,0:T(8,128)(2,1)} %q_any.1, bf16[256,1536]{1,0:T(8,128)(2,1)} %k_any.1, bf16[256,1536]{1,0:T(8,128)(2,1)} %v_any.1, bf16[256,1536]{1,0:T(8,128)(2,1)} %res_any.1, s32[1]{0:T(128)S(6)} %copy.11.levels, f32[50,1536]{1,0:T(8,128)} %gate_any.1, s32[1,7,4,4]{3,2,1,0:T(4,128)} %copy.9.mask_any, ...), custom_call_target="tpu_custom_call" | custom-call | flops 6845104128 | bytes 6291456 | tf_op jit(solution)/shard_map/pallas_call | solution.py:388
  72.4 2.1 %copy.12 = bf16[256,1536]{1,0:T(8,128)(2,1)} copy(bf16[256,1536]{1,0:T(8,128)(2,1)} %shard_map.82) | data formatting | bytes 1572864
